TPU v7x, 128 devices: a whole 4x4x4 slice. The times are simulated.
128 devices in a mesh: row: 16 (over y_lo, x, core), col: 8 (over y_hi, z).
Axes of the slice: x: 4, y: 4 (y_hi: 2, y_lo: 2; y = y_hi * 2 + y_lo), z: 4, core: 2. Of those that a mesh axis runs over, the one named last changes fastest.
Arguments:
- resid: bfloat16 [2048, 5120], P('row', 'col'), may hold values from -160 to 160
- queries: bfloat16 [2048, 5120], P('row', 'col'), may hold values from -24 to 24
- keys: bfloat16 [2048, 5120], P('row', 'col'), may hold values from -24 to 24
- values: bfloat16 [2048, 5120], P('row', 'col'), may hold values from -6 to 6
- doc_ids: int32 [2048], replicated, may hold values from 0 to 7, never falling along the last dimension, each value on 1 to 1536 neighbouring positions
- norm_gain: float32 [5120], replicated, may hold values from 0.1 to 1.9
- expert_ids: int32 [2048, 6], P('row'), may hold values from 0 to 31, all different within a row; in each aligned block of 128 rows (0 to 127, 128 to 255, ...) at most 32 rows name the same one
- gate_levels: int32 [2048, 6], P('row'), may hold values from 1 to 64
- w_gate: bfloat16 [32, 1536, 5120], P('row', 'col'), may hold values from -0.078125 to 0.078125
- w_up: bfloat16 [32, 1536, 5120], P('row', 'col'), may hold values from -0.078125 to 0.078125
- w_down: bfloat16 [32, 1536, 5120], P('row', 'col'), may hold values from -0.15625 to 0.15625
- cotangent: bfloat16 [2048, 5120], P('row', 'col'), may hold values from -6 to 6
Outputs:
- d_normed: bfloat16 [2048, 5120], P('row', 'col')
- d_w_gate: bfloat16 [32, 1536, 5120], P('row', 'col')
- d_w_up: bfloat16 [32, 1536, 5120], P('row', 'col')
- d_w_down: bfloat16 [32, 1536, 5120], P('row', 'col')
Inputs may be any that keep to these rules, and one draw needn't show every extreme that they name: `doc_ids`: document numbers never fall along the tokens; one document spans exactly 1536 tokens. `expert_ids`: each token names 6 different experts. In each aligned block of 128 tokens (the tokens of one row index) no expert is named by more than 32 tokens, a bound that some block reaches.
All inputs are finite; a program needn't handle non-finite values.
Results may differ from a plain program's by a relative error of at most 0.017.
Values may be sent and summed in bfloat16 or wider, within the bound.
No kernel may reach another device: no remote copies, remote signals or barrier semaphores. Data moves between devices by JAX's collectives and lax.ppermute only.
A program may use at most 256 MiB of HBM per device.

v0:
```python
import math
import jax
import jax.numpy as jnp
from jax import lax
from jax.sharding import PartitionSpec as P

HEAD_DIM = 128
TOP = 6
WINDOW = 1024


def from_behind(x, axis, by):
    devices = lax.axis_size(axis)
    pairs = [(i, i + by) for i in range(devices) if 0 <= i + by < devices]
    return lax.ppermute(x, axis, pairs)


def body(
    resid,
    queries,
    keys,
    values,
    doc_ids,
    norm_gain,
    expert_ids,
    gate_levels,
    w_gate,
    w_up,
    w_down,
    cotangent,
):
    tok_rows, feat_width = queries.shape
    row_index = lax.axis_index("row")
    row_count = lax.axis_size("row")
    reach_count = WINDOW // tok_rows
    key_list = []
    value_list = []
    for distance in range(reach_count, 0, -1):
        moved_keys, moved_values = from_behind((keys, values), "row", distance)
        key_list.append(moved_keys)
        value_list.append(moved_values)
    all_keys = jnp.concatenate(key_list + [keys], axis=0)
    all_values = jnp.concatenate(value_list + [values], axis=0)
    key_total = (reach_count + 1) * tok_rows
    padded_docs = jnp.concatenate([jnp.full((reach_count * tok_rows,), -1, jnp.int32), doc_ids])
    key_docs = lax.dynamic_slice_in_dim(padded_docs, row_index * tok_rows, key_total)
    query_docs = lax.dynamic_slice_in_dim(doc_ids, row_index * tok_rows, tok_rows)
    query_pos = row_index * tok_rows + jnp.arange(tok_rows, dtype=jnp.int32)
    key_pos = (row_index - reach_count) * tok_rows + jnp.arange(key_total, dtype=jnp.int32)
    pos_delta = query_pos[:, None] - key_pos[None, :]
    allowed = (pos_delta >= 0) & (pos_delta < WINDOW) & (query_docs[:, None] == key_docs[None, :])
    heads_here = feat_width // HEAD_DIM
    query_heads = queries.reshape(tok_rows, heads_here, HEAD_DIM)
    key_heads = all_keys.reshape(key_total, heads_here, HEAD_DIM)
    value_heads = all_values.reshape(key_total, heads_here, HEAD_DIM)
    scores = jnp.einsum(
        "qhd,khd->hqk", query_heads, key_heads, preferred_element_type=jnp.float32
    ) * (1.0 / math.sqrt(HEAD_DIM))
    scores = jnp.where(allowed[None], scores, -1e30)
    top_score = jnp.max(scores, axis=2, keepdims=True)
    weights = jnp.exp(scores - top_score)
    probs = (weights / jnp.sum(weights, axis=2, keepdims=True)).astype(jnp.bfloat16)
    attention = jnp.einsum(
        "hqk,khd->qhd", probs, value_heads, preferred_element_type=jnp.float32
    ).reshape(tok_rows, feat_width)
    hidden_in = (resid.astype(jnp.float32) + attention).astype(jnp.bfloat16)
    local_experts = w_gate.shape[0]
    experts_total = local_experts * row_count
    capacity = 4 * tok_rows * TOP // (3 * experts_total)
    flat_ids = expert_ids.reshape(-1)
    matches = (flat_ids[:, None] == jnp.arange(experts_total, dtype=jnp.int32)[None, :]).astype(
        jnp.int32
    )
    slot_index = jnp.sum(matches * jnp.cumsum(matches, axis=0), axis=1) - 1
    target_index = flat_ids * capacity + slot_index
    assign_table = (
        jnp.full((experts_total * capacity,), tok_rows * TOP, jnp.int32)
        .at[target_index]
        .set(jnp.arange(tok_rows * TOP, dtype=jnp.int32))
    )
    token_table = assign_table // TOP
    gate_weights = gate_levels.reshape(-1).astype(jnp.float32) / 64.0
    full_hidden, full_grads = (
        lax.all_gather(hidden_in, "col", axis=1, tiled=True),
        lax.all_gather(cotangent, "col", axis=1, tiled=True),
    )
    widened = full_hidden.astype(jnp.float32)
    inv_rms = lax.rsqrt(jnp.mean(widened * widened, axis=1, keepdims=True) + 1e-05)
    normed = (widened * inv_rms * norm_gain[None, :]).astype(jnp.bfloat16)
    feat_count = normed.shape[1]
    zero_row = jnp.zeros((1, feat_count), jnp.bfloat16)
    scaled_grad = (
        gate_weights[:, None] * jnp.repeat(full_grads, TOP, axis=0).astype(jnp.float32)
    ).astype(jnp.bfloat16)
    routed_in = jnp.concatenate([normed, zero_row], axis=0)[token_table].reshape(
        row_count, local_experts, capacity, feat_count
    )
    routed_grad = jnp.concatenate([scaled_grad, zero_row], axis=0)[assign_table].reshape(
        row_count, local_experts, capacity, feat_count
    )
    recv_in, recv_grad = (
        lax.all_to_all(routed_in, "row", split_axis=0, concat_axis=0, tiled=True),
        lax.all_to_all(routed_grad, "row", split_axis=0, concat_axis=0, tiled=True),
    )
    pre_gate = jnp.einsum("secd,efd->secf", recv_in, w_gate, preferred_element_type=jnp.float32)
    pre_up = jnp.einsum("secd,efd->secf", recv_in, w_up, preferred_element_type=jnp.float32)
    gate_sigmoid = jax.nn.sigmoid(pre_gate)
    silu_gate = pre_gate * gate_sigmoid
    act = (silu_gate * pre_up).astype(jnp.bfloat16)
    grad_act = jnp.einsum("secd,efd->secf", recv_grad, w_down, preferred_element_type=jnp.float32)
    grad_gate = (grad_act * pre_up * gate_sigmoid * (1.0 + pre_gate * (1.0 - gate_sigmoid))).astype(
        jnp.bfloat16
    )
    grad_up = (grad_act * silu_gate).astype(jnp.bfloat16)
    d_w_down = jnp.einsum(
        "secf,secd->efd", act, recv_grad, preferred_element_type=jnp.float32
    ).astype(jnp.bfloat16)
    d_w_gate = jnp.einsum(
        "secf,secd->efd", grad_gate, recv_in, preferred_element_type=jnp.float32
    ).astype(jnp.bfloat16)
    d_w_up = jnp.einsum(
        "secf,secd->efd", grad_up, recv_in, preferred_element_type=jnp.float32
    ).astype(jnp.bfloat16)
    block_terms = jnp.einsum(
        "secf,efd->secd", grad_gate, w_gate, preferred_element_type=jnp.float32
    )
    block_terms = block_terms + jnp.einsum(
        "secf,efd->secd", grad_up, w_up, preferred_element_type=jnp.float32
    )
    block_terms = block_terms.astype(jnp.bfloat16)
    returned = lax.all_to_all(block_terms, "row", split_axis=0, concat_axis=0, tiled=True)
    flat_rows = returned.reshape(experts_total * capacity, -1)[target_index]
    d_normed = lax.psum_scatter(
        jnp.sum(flat_rows.astype(jnp.float32).reshape(tok_rows, TOP, -1), axis=1).astype(
            jnp.bfloat16
        ),
        "col",
        scatter_dimension=1,
        tiled=True,
    )
    return (d_normed, d_w_gate, d_w_up, d_w_down)


def solution(mesh):
    return jax.shard_map(
        body,
        mesh=mesh,
        in_specs=(
            P("row", "col"),
            P("row", "col"),
            P("row", "col"),
            P("row", "col"),
            P(),
            P(),
            P("row", None),
            P("row", None),
            P("row", "col", None),
            P("row", "col", None),
            P("row", "col", None),
            P("row", "col"),
        ),
        out_specs=(
            P("row", "col"),
            P("row", "col", None),
            P("row", "col", None),
            P("row", "col", None),
        ),
        check_vma=False,
    )
```

profile of v0, /device:TPU:0, one launch (start us, length us, event | category | flops | bytes accessed | tf_op | source)
XLA Modules:
  0.0 821.8 jit_solution(7680869357388876416)
XLA Ops:
  54.6 8.0 collective-permute-start.9
  104.5 48.0 %all-gather.5.cloned.1.call-done = bf16[128,5120]{1,0:T(8,128)(2,1)} async-done(((bf16[128,640]{1,0:T(8,128)(2,1)}), bf16[128,5120]{1,0:T(8,128)(2,1)}) %all-gather.5.cloned.1.call-update) | async-done | bytes 1310736 | tf_op jit(solution)/shard_map/all_gather | solution.py:84
  156.1 8.7 %gather_fusion.1 = bf16[1024,5120]{1,0:T(8,128)(2,1)} fusion(bf16[129,5120]{1,0:T(8,128)(2,1)S(1)} %concatenate.19, s32[1024]{0:T(1024)S(1)} %get-tuple-element.7), kind=kCustom, calls=%fused_computation.1 | custom fusion | bytes 20975616 | tf_op jit(solution)/shard_map/gather | solution.py:95
  169.8 13.7 %all-gather.3.cloned.1.call-start = ((), (), s32[]{:S(2)}) async-start(), calls=%async_computation.4 | async-start | bytes 1474560 | tf_op jit(solution)/shard_map/all_gather | solution.py:85
  183.8 110.6 %all-gather.3.cloned.1.call-done = bf16[128,5120]{1,0:T(8,128)(2,1)} async-done(((bf16[128,640]{1,0:T(8,128)(2,1)}), bf16[128,5120]{1,0:T(8,128)(2,1)}) %all-gather.3.cloned.1.call-update) | async-done | bytes 1310736 | tf_op jit(solution)/shard_map/all_gather | solution.py:85
  294.4 8.8 %broadcast_in_dim.20 = f32[128,6,5120]{2,1,0:T(8,128)} broadcast(bf16[128,5120]{1,0:T(8,128)(2,1)} %all-gather.3.cloned.1.call-done), dimensions={0,2} | broadcast | bytes 17039360 | tf_op jit(solution)/shard_map/broadcast_in_dim | solution.py:93
  303.2 18.4 %convert_element_type.67 = f32[768,5120]{1,0:T(8,128)} reshape(f32[128,6,5120]{2,1,0:T(8,128)} %broadcast_in_dim.20) | data formatting | bytes 31457280 | tf_op jit(solution)/shard_map/convert_element_type | solution.py:93
  331.8 22.8 %gather_fusion = bf16[1024,5120]{1,0:T(8,128)(2,1)} fusion(bf16[769,5120]{1,0:T(8,128)(2,1)} %concatenate.15, s32[1024]{0:T(1024)S(1)} %get-tuple-element.6), kind=kCustom, calls=%fused_computation | custom fusion | bytes 20975616 | tf_op jit(solution)/shard_map/gather | solution.py:98
  354.6 16.2 %all-to-all-start = ((bf16[16,2,32,5120]{3,2,1,0:T(8,128)(2,1)}), bf16[16,2,32,5120]{3,2,1,0:T(8,128)(2,1)}, u32[]{:S(2)}, u32[]{:S(2)}) async-start(bf16[16,2,32,5120]{3,2,1,0:T(8,128)(2,1)} %bitcast.96), calls=%async_computation | async-start | bytes 20971520 | tf_op jit(solution)/shard_map/all_to_all | solution.py:103
  370.8 7.0 fusion.33
  377.7 7.8 fusion.28
  385.6 126.2 %all-to-all-done = bf16[16,2,32,5120]{3,2,1,0:T(8,128)(2,1)} async-done(((bf16[16,2,32,5120]{3,2,1,0:T(8,128)(2,1)}), bf16[16,2,32,5120]{3,2,1,0:T(8,128)(2,1)}, u32[]{:S(2)}, u32[]{:S(2)}) %all-to-all-start) | async-done | bytes 10485792 | tf_op jit(solution)/shard_map/all_to_all | solution.py:103
  511.8 8.7 %multiply_convert_fusion.2 = (bf16[16,2,32,192]{3,2,0,1:T(8,128)(2,1)S(1)}, bf16[16,2,32,192]{3,2,0,1:T(8,128)(2,1)S(1)}) fusion(f32[16,2,32,192]{3,2,0,1:T(8,128)S(1)} %fusion.33, f32[16,2,32,192]{3,2,0,1:T(8,128)} %fusion.28, bf16[2,192,5120]{2,1,0:T(8,128)(2,1)} %param.22, bf16[16,2,32,5120]{3,2,1,0:T(8,128)(2,1)} %all-to-all-done), kind=kOutput, calls=%fused_computation.43 | convolution fusion | flops 2015821824 | bytes 16777216 | tf_op jit(solution)/shard_map/secd,efd->secf/dot_general | solution.py:110
  520.6 8.5 %fusion.15 = f32[2,16,32,5120]{3,2,1,0:T(8,128)} fusion(bf16[16,2,32,192]{3,2,0,1:T(8,128)(2,1)S(1)} %get-tuple-element.5, bf16[2,192,5120]{2,1,0:T(8,128)(2,1)S(1)} %copy-done), kind=kOutput, calls=%fused_computation.22 | convolution fusion | flops 2013265920 | bytes 25296896 | tf_op jit(solution)/shard_map/secf,efd->secd/dot_general | solution.py:124
  529.1 13.1 %fusion.5 = bf16[16,2,32,5120]{3,2,0,1:T(8,128)(2,1)} fusion(f32[2,16,32,5120]{3,2,1,0:T(8,128)} %fusion.15, bf16[16,2,32,192]{3,2,0,1:T(8,128)(2,1)S(1)} %get-tuple-element.4, bf16[2,192,5120]{2,1,0:T(8,128)(2,1)} %param.21), kind=kOutput, calls=%fused_computation.11 | convolution fusion | flops 2023751680 | bytes 35782656 | tf_op jit(solution)/shard_map/secf,efd->secd/dot_general | solution.py:127
  542.2 9.0 %copy.66 = bf16[16,2,32,5120]{3,2,1,0:T(8,128)(2,1)} copy(bf16[16,2,32,5120]{3,2,0,1:T(8,128)(2,1)} %fusion.5) | data formatting | bytes 20971520 | tf_op jit(solution)/shard_map/convert_element_type | solution.py:130
  556.1 8.2 bitcast_convert_fusion.1
  564.2 132.6 %all-to-all-done.2 = bf16[16,2,32,5120]{3,2,1,0:T(8,128)(2,1)} async-done(((bf16[16,2,32,5120]{3,2,1,0:T(8,128)(2,1)}), bf16[16,2,32,5120]{3,2,1,0:T(8,128)(2,1)}, u32[]{:S(2)}, u32[]{:S(2)}) %all-to-all-start.2) | async-done | bytes 10485792 | tf_op jit(solution)/shard_map/all_to_all | solution.py:131
  696.9 20.3 %gather_fusion.2 = bf16[768,5120]{1,0:T(8,128)(2,1)} fusion(bf16[1024,5120]{1,0:T(8,128)(2,1)} %bitcast.20, s32[1024]{0:T(1024)S(1)} %pad_clamp_fusion), kind=kCustom, calls=%fused_computation.2 | custom fusion | bytes 15731712 | tf_op jit(solution)/shard_map/gather | solution.py:132
  717.1 13.1 %gather.14 = bf16[128,6,5120]{2,1,0:T(8,128)(2,1)} reshape(bf16[768,5120]{1,0:T(8,128)(2,1)} %gather_fusion.2) | data formatting | bytes 15728640 | tf_op jit(solution)/shard_map/gather | solution.py:132
  730.2 10.4 %reduce_sum.42 = bf16[128,5120]{1,0:T(8,128)(2,1)S(1)} reduce(bf16[128,6,5120]{2,1,0:T(8,128)(2,1)} %gather.14, bf16[]{:T(256)} %constant.25.clone.1), dimensions={1}, to_apply=%region_7.8 | reduce | flops 3276800 | bytes 9175042 | tf_op jit(solution)/shard_map/reduce_sum | solution.py:134
  742.4 8.2 %bitcast_convert_fusion.2 = bf16[2,192,5120]{2,1,0:T(8,128)(2,1)} fusion(bf16[16,2,32,192]{3,2,0,1:T(8,128)(2,1)S(1)} %get-tuple-element.5, bf16[16,2,32,5120]{3,2,1,0:T(8,128)(2,1)} %all-to-all-done.1), kind=kOutput, calls=%fused_computation.14 | convolution fusion | flops 2015232000 | bytes 14811136 | tf_op jit(solution)/shard_map/secf,secd->efd/dot_general | solution.py:118
  750.6 8.4 %bitcast_convert_fusion = bf16[2,192,5120]{2,1,0:T(8,128)(2,1)} fusion(bf16[16,2,32,5120]{3,2,1,0:T(8,128)(2,1)} %all-to-all-done, f32[16,2,32,192]{3,2,0,1:T(8,128)S(1)} %copy-done.8, f32[16,2,32,192]{3,2,0,1:T(8,128)S(1)} %fusion.33), kind=kOutput, calls=%fused_computation.12 | convolution fusion | flops 2016411648 | bytes 15990784 | tf_op jit(solution)/shard_map/secf,secd->efd/dot_general | solution.py:115
  759.0 54.4 %reduce-scatter.4.cloned.1.call-done = bf16[640,128]{1,0:T(8,128)(2,1)} async-done(((bf16[5120,128]{1,0:T(8,128)(2,1)}), bf16[640,128]{1,0:T(8,128)(2,1)}) %reduce-scatter.4.cloned.1.call-update) | async-done | bytes 163856
  (114 shorter events, 116.1 us)
Async XLA Ops:
  7.2 60.0 %copy-start.3 = (bf16[128,640]{1,0:T(8,128)(2,1)S(1)}, bf16[128,640]{1,0:T(8,128)(2,1)}, u32[]{:S(2)}) copy-start(bf16[128,640]{1,0:T(8,128)(2,1)} %param.15) | copy-start | bytes 491524
  7.2 145.4 %all-gather.5.cloned.1.call-start = ((), (), s32[]{:S(2)}) async-start(), calls=%async_computation.5 | async-start | bytes 1474560 | tf_op jit(solution)/shard_map/all_gather | solution.py:84
  8.3 81.8 %collective-permute-start.15 = (bf16[128,640]{0,1:T(8,128)(2,1)S(1)}, bf16[128,640]{0,1:T(8,128)(2,1)S(1)}, u32[]{:S(2)}, u32[]{:S(2)}) collective-permute-start(bf16[128,640]{0,1:T(8,128)(2,1)S(1)} %copy.50), channel_id=1, source_target_pairs={{0,8},{8,16},{16,24},{24,32},{32,40},{40,48},{48,56},{56,64},{64,7... | collective-permute-start | bytes 491528 | tf_op jit(solution)/shard_map/ppermute | solution.py:15
  9.6 79.8 %collective-permute-start.14 = (bf16[128,640]{0,1:T(8,128)(2,1)S(1)}, bf16[128,640]{0,1:T(8,128)(2,1)S(1)}, u32[]{:S(2)}, u32[]{:S(2)}) collective-permute-start(bf16[128,640]{0,1:T(8,128)(2,1)S(1)} %copy.50), channel_id=1, source_target_pairs={{0,16},{8,24},{16,32},{24,40},{32,48},{40,56},{48,64},{56,72},{64,... | collective-permute-start | bytes 491528 | tf_op jit(solution)/shard_map/ppermute | solution.py:15
  13.7 74.1 %collective-permute-start.13 = (bf16[128,640]{0,1:T(8,128)(2,1)S(1)}, bf16[128,640]{0,1:T(8,128)(2,1)S(1)}, u32[]{:S(2)}, u32[]{:S(2)}) collective-permute-start(bf16[128,640]{0,1:T(8,128)(2,1)S(1)} %copy.50), channel_id=1, source_target_pairs={{0,24},{8,32},{16,40},{24,48},{32,56},{40,64},{48,72},{56,80},{64,... | collective-permute-start | bytes 491528 | tf_op jit(solution)/shard_map/ppermute | solution.py:15
  17.8 13.0 %collective-permute-start.1 = (bf16[128,640]{1,0:T(8,128)(2,1)}, bf16[128,640]{1,0:T(8,128)(2,1)S(1)}, u32[]{:S(2)}, u32[]{:S(2)}) collective-permute-start(bf16[128,640]{1,0:T(8,128)(2,1)} %param.15), channel_id=1, source_target_pairs={{0,56},{8,64},{16,72},{24,80},{32,88},{40,96},{48,104},{56,112},{6... | collective-permute-start | bytes 491528 | tf_op jit(solution)/shard_map/ppermute | solution.py:15
  22.5 7.0 collective-permute-start
  29.5 7.9 collective-permute-start.2
  30.8 11.1 %collective-permute-start.3 = (bf16[128,640]{1,0:T(8,128)(2,1)}, bf16[128,640]{1,0:T(8,128)(2,1)S(1)}, u32[]{:S(2)}, u32[]{:S(2)}) collective-permute-start(bf16[128,640]{1,0:T(8,128)(2,1)} %param.15), channel_id=1, source_target_pairs={{0,40},{8,48},{16,56},{24,64},{32,72},{40,80},{48,88},{56,96},{64,... | collective-permute-start | bytes 491528 | tf_op jit(solution)/shard_map/ppermute | solution.py:15
  37.4 8.5 %collective-permute-start.4 = (bf16[128,640]{1,0:T(8,128)(2,1)}, bf16[128,640]{1,0:T(8,128)(2,1)S(1)}, u32[]{:S(2)}, u32[]{:S(2)}) collective-permute-start(bf16[128,640]{1,0:T(8,128)(2,1)} %param.15), channel_id=1, source_target_pairs={{0,32},{8,40},{16,48},{24,56},{32,64},{40,72},{48,80},{56,88},{64,... | collective-permute-start | bytes 491528 | tf_op jit(solution)/shard_map/ppermute | solution.py:15
  41.9 8.4 %collective-permute-start.5 = (bf16[128,640]{1,0:T(8,128)(2,1)}, bf16[128,640]{1,0:T(8,128)(2,1)S(1)}, u32[]{:S(2)}, u32[]{:S(2)}) collective-permute-start(bf16[128,640]{1,0:T(8,128)(2,1)} %param.15), channel_id=1, source_target_pairs={{0,24},{8,32},{16,40},{24,48},{32,56},{40,64},{48,72},{56,80},{64,... | collective-permute-start | bytes 491528 | tf_op jit(solution)/shard_map/ppermute | solution.py:15
  46.0 8.6 %collective-permute-start.6 = (bf16[128,640]{1,0:T(8,128)(2,1)}, bf16[128,640]{1,0:T(8,128)(2,1)S(1)}, u32[]{:S(2)}, u32[]{:S(2)}) collective-permute-start(bf16[128,640]{1,0:T(8,128)(2,1)} %param.15), channel_id=1, source_target_pairs={{0,16},{8,24},{16,32},{24,40},{32,48},{40,56},{48,64},{56,72},{64,... | collective-permute-start | bytes 491528 | tf_op jit(solution)/shard_map/ppermute | solution.py:15
  50.3 12.3 %collective-permute-start.7 = (bf16[128,640]{1,0:T(8,128)(2,1)}, bf16[128,640]{1,0:T(8,128)(2,1)S(1)}, u32[]{:S(2)}, u32[]{:S(2)}) collective-permute-start(bf16[128,640]{1,0:T(8,128)(2,1)} %param.15), channel_id=1, source_target_pairs={{0,8},{8,16},{16,24},{24,32},{32,40},{40,48},{48,56},{56,64},{64,7... | collective-permute-start | bytes 491528 | tf_op jit(solution)/shard_map/ppermute | solution.py:15
  54.6 19.2 %collective-permute-start.9 = (bf16[128,640]{0,1:T(8,128)(2,1)S(1)}, bf16[128,640]{0,1:T(8,128)(2,1)S(1)}, u32[]{:S(2)}, u32[]{:S(2)}) collective-permute-start(bf16[128,640]{0,1:T(8,128)(2,1)S(1)} %copy.50), channel_id=1, source_target_pairs={{0,56},{8,64},{16,72},{24,80},{32,88},{40,96},{48,104},{56,112},{6... | collective-permute-start | bytes 491528 | tf_op jit(solution)/shard_map/ppermute | solution.py:15
  62.6 9.2 %collective-permute-start.8 = (bf16[128,640]{0,1:T(8,128)(2,1)S(1)}, bf16[128,640]{0,1:T(8,128)(2,1)S(1)}, u32[]{:S(2)}, u32[]{:S(2)}) collective-permute-start(bf16[128,640]{0,1:T(8,128)(2,1)S(1)} %copy.50), channel_id=1, source_target_pairs={{0,64},{8,72},{16,80},{24,88},{32,96},{40,104},{48,112},{56,120},{... | collective-permute-start | bytes 491528 | tf_op jit(solution)/shard_map/ppermute | solution.py:15
  71.8 7.7 collective-permute-start.10
  73.8 11.2 %collective-permute-start.11 = (bf16[128,640]{0,1:T(8,128)(2,1)S(1)}, bf16[128,640]{0,1:T(8,128)(2,1)S(1)}, u32[]{:S(2)}, u32[]{:S(2)}) collective-permute-start(bf16[128,640]{0,1:T(8,128)(2,1)S(1)} %copy.50), channel_id=1, source_target_pairs={{0,40},{8,48},{16,56},{24,64},{32,72},{40,80},{48,88},{56,96},{64,... | collective-permute-start | bytes 491528 | tf_op jit(solution)/shard_map/ppermute | solution.py:15
  79.5 7.7 collective-permute-start.12
  97.3 56.9 %copy-start.5 = (f32[5120]{0:T(1024)S(1)}, f32[5120]{0:T(1024)}, u32[]{:S(2)}) copy-start(f32[5120]{0:T(1024)} %param.17) | copy-start | bytes 61444
  164.8 189.8 %all-to-all-start.1 = ((bf16[16,2,32,5120]{3,2,1,0:T(8,128)(2,1)}), bf16[16,2,32,5120]{3,2,1,0:T(8,128)(2,1)}, u32[]{:S(2)}, u32[]{:S(2)}) async-start(bf16[16,2,32,5120]{3,2,1,0:T(8,128)(2,1)} %bitcast.95), calls=%async_computation.1 | async-start | bytes 20971520 | tf_op jit(solution)/shard_map/all_to_all | solution.py:102
  169.8 124.6 %all-gather.3.cloned.1.call-start = ((), (), s32[]{:S(2)}) async-start(), calls=%async_computation.4 | async-start | bytes 1474560 | tf_op jit(solution)/shard_map/all_gather | solution.py:85
  354.6 157.2 %all-to-all-start = ((bf16[16,2,32,5120]{3,2,1,0:T(8,128)(2,1)}), bf16[16,2,32,5120]{3,2,1,0:T(8,128)(2,1)}, u32[]{:S(2)}, u32[]{:S(2)}) async-start(bf16[16,2,32,5120]{3,2,1,0:T(8,128)(2,1)} %bitcast.96), calls=%async_computation | async-start | bytes 20971520 | tf_op jit(solution)/shard_map/all_to_all | solution.py:103
  551.2 145.7 %all-to-all-start.2 = ((bf16[16,2,32,5120]{3,2,1,0:T(8,128)(2,1)}), bf16[16,2,32,5120]{3,2,1,0:T(8,128)(2,1)}, u32[]{:S(2)}, u32[]{:S(2)}) async-start(bf16[16,2,32,5120]{3,2,1,0:T(8,128)(2,1)} %copy.66), calls=%async_computation.2 | async-start | bytes 20971520 | tf_op jit(solution)/shard_map/all_to_all | solution.py:131
  556.0 257.4 %reduce-scatter.4.cloned.1.call-start = ((), (), s32[]{:S(2)}) async-start(), calls=%async_computation.6 | async-start | bytes 1474560
  (7 other events, 52.7 us)
Sparse Core Ops, SparseCore 0:
  98.4 54.1 all-gather.4
  183.7 110.6 all-gather.2
  742.5 70.8 reduce-scatter.3
where the time goes:
time: 831 us; the launch traced here: 822 us
  waiting for transfers between devices  481 us (58%)
  local copies, waits for them, and re-layouts  124 us (15%)
  starting transfers between devices  102 us (12%)
  matrix products  75.7 us (9%)
  other arithmetic  25 us (3%)
  between operations  14.5 us (2%)
    all_to_all x1, waiting for transfers between devices, body(): lax.all_to_all(block_terms, 'row', split_axis=0, concat_axis=0, tiled=True)  133 us
    all_to_all x1, waiting for transfers between devices, body(): lax.all_to_all(routed_grad, 'row', split_axis=0, concat_axis=0, tiled=True)  126 us
    all_gather x1, waiting for transfers between devices, body(): lax.all_gather(cotangent, 'col', axis=1, tiled=True)  111 us
    ppermute x16, starting transfers between devices, from_behind(): return lax.ppermute(x, axis, pairs)  62.1 us
    unnamed x4, waiting for transfers between devices  54.4 us
    all_gather x1, waiting for transfers between devices, body(): lax.all_gather(hidden_in, 'col', axis=1, tiled=True)  48 us
    gather x2, local copies, waits for them, and re-layouts, body(): flat_rows = returned.reshape(experts_total * capacity, -1)[target_index]  33.4 us
    gather x1, local copies, waits for them, and re-layouts, body(): jnp.concatenate([scaled_grad, zero_row], axis=0)[assign_table]  22.8 us
  transfers between devices with their start and end apart: 22, of which 10 were waited for; matrix products, arithmetic and copies ran while one was open for 14% of the time, Pallas kernels for 0%

commit v1 on v0

--- a/solution.py
+++ b/solution.py
@@ -82,7 +82,9 @@
     gate_weights = gate_levels.reshape(-1).astype(jnp.float32) / 64.0
     full_hidden, full_grads = (
         lax.all_gather(hidden_in, "col", axis=1, tiled=True),
-        lax.all_gather(cotangent, "col", axis=1, tiled=True),
+        jnp.concatenate(
+            lax.all_to_all(jnp.stack([cotangent] * lax.axis_size("col")), "col", 0, 0), axis=1
+        ),
     )
     widened = full_hidden.astype(jnp.float32)
     inv_rms = lax.rsqrt(jnp.mean(widened * widened, axis=1, keepdims=True) + 1e-05)

time: 831 us -> 796 us (0.958)
  waiting for transfers between devices: 481 us -> 442 us
    all_gather x1 -> x0, waiting for transfers between devices: 111 us -> none  [body(): lax.all_gather(cotangent, 'col', axis=1, tiled=True)]
    all_to_all x1, waiting for transfers between devices: 0.01 us -> 74.7 us  [body(): lax.all_to_all(routed_in, 'row', split_axis=0, concat_axis=0, tiled=True)]
    all_to_all x1, starting transfers between devices: 4.99 us -> 19.2 us  [body(): lax.all_to_all(routed_in, 'row', split_axis=0, concat_axis=0, tiled=True)]
    all_gather x1 -> x0, starting transfers between devices: 13.7 us -> none  [body(): lax.all_gather(cotangent, 'col', axis=1, tiled=True)]
    all_to_all x1, starting transfers between devices: 16.2 us -> 4.89 us  [body(): lax.all_to_all(routed_grad, 'row', split_axis=0, concat_axis=0, tiled=True)]
    convert_element_type x1 -> x2, local copies, waits for them, and re-layouts: 18.4 us -> 20.5 us  [body(): jnp.repeat(full_grads, TOP, axis=0).astype(jnp.float32)]
    unnamed x4 -> x3, waiting for transfers between devices: 54.4 us -> 55.7 us
  transfers between devices with their start and end apart: 22 -> 22, of which waited for: 10 -> 10; matrix products, arithmetic and copies ran while one was open for 14% -> 17% of each run, Pallas kernels for 0% -> 0%
where the time goes in v1:
time: 796 us; the launch traced here: 787 us
  waiting for transfers between devices  442 us (56%)
  local copies, waits for them, and re-layouts  129 us (16%)
  starting transfers between devices  99.2 us (12%)
  matrix products  75.7 us (10%)
  other arithmetic  26.5 us (3%)
  between operations  14.9 us (2%)
    all_to_all x1, waiting for transfers between devices, body(): lax.all_to_all(block_terms, 'row', split_axis=0, concat_axis=0, tiled=True)  133 us
    all_to_all x1, waiting for transfers between devices, body(): lax.all_to_all(routed_grad, 'row', split_axis=0, concat_axis=0, tiled=True)  126 us
    all_to_all x1, waiting for transfers between devices, body(): lax.all_to_all(routed_in, 'row', split_axis=0, concat_axis=0, tiled=True)  74.7 us
    ppermute x16, starting transfers between devices, from_behind(): return lax.ppermute(x, axis, pairs)  62.1 us
    unnamed x3, waiting for transfers between devices  55.7 us
    all_gather x1, waiting for transfers between devices, body(): lax.all_gather(hidden_in, 'col', axis=1, tiled=True)  43.8 us
    gather x2, local copies, waits for them, and re-layouts, body(): flat_rows = returned.reshape(experts_total * capacity, -1)[target_index]  33.4 us
    gather x1, local copies, waits for them, and re-layouts, body(): jnp.concatenate([scaled_grad, zero_row], axis=0)[assign_table]  22.8 us
  transfers between devices with their start and end apart: 22, of which 10 were waited for; matrix products, arithmetic and copies ran while one was open for 17% of the time, Pallas kernels for 0%

profile of v1, /device:TPU:0, one launch (start us, length us, event | category | flops | bytes accessed | tf_op | source)
XLA Modules:
  0.0 787.1 jit_solution(3684815510584297414)
XLA Ops:
  54.6 8.0 %collective-permute-start.9 = (bf16[128,640]{0,1:T(8,128)(2,1)S(1)}, bf16[128,640]{0,1:T(8,128)(2,1)S(1)}, u32[]{:S(2)}, u32[]{:S(2)}) collective-permute-start(bf16[128,640]{0,1:T(8,128)(2,1)S(1)} %copy.79), channel_id=1, source_target_pairs={{0,56},{8,64},{16,72},{24,80},{32,88},{40,96},{48,104},{56,112},{6... | collective-permute-start | bytes 491528 | tf_op jit(solution)/shard_map/ppermute | solution.py:15
  99.4 7.9 %all-to-all-start = ((bf16[8,128,640]{2,1,0:T(8,128)(2,1)}), bf16[8,128,640]{2,1,0:T(8,128)(2,1)S(1)}, u32[]{:S(2)}, u32[]{:S(2)}) async-start(bf16[8,128,640]{2,1,0:T(8,128)(2,1)} %stack.2), calls=%async_computation | async-start | bytes 2621440 | tf_op jit(solution)/shard_map/all_to_all | solution.py:86
  113.7 43.8 %all-gather.2.cloned.1.call-done = bf16[128,5120]{1,0:T(8,128)(2,1)} async-done(((bf16[128,640]{1,0:T(8,128)(2,1)}), bf16[128,5120]{1,0:T(8,128)(2,1)}) %all-gather.2.cloned.1.call-update) | async-done | bytes 1310736 | tf_op jit(solution)/shard_map/all_gather | solution.py:84
  160.9 8.7 %gather_fusion.1 = bf16[1024,5120]{1,0:T(8,128)(2,1)} fusion(bf16[129,5120]{1,0:T(8,128)(2,1)S(1)} %concatenate.19, s32[1024]{0:T(1024)S(1)} %get-tuple-element.7), kind=kCustom, calls=%fused_computation.1 | custom fusion | bytes 20975616 | tf_op jit(solution)/shard_map/gather | solution.py:97
  169.7 19.2 %all-to-all-start.2 = ((bf16[16,2,32,5120]{3,2,1,0:T(8,128)(2,1)}), bf16[16,2,32,5120]{3,2,1,0:T(8,128)(2,1)}, u32[]{:S(2)}, u32[]{:S(2)}) async-start(bf16[16,2,32,5120]{3,2,1,0:T(8,128)(2,1)} %bitcast.98), calls=%async_computation.2 | async-start | bytes 20971520 | tf_op jit(solution)/shard_map/all_to_all | solution.py:104
  194.2 9.1 %broadcast_in_dim.20 = f32[128,6,5120]{2,1,0:T(8,128)} broadcast(f32[128,5120]{1,0:T(8,128)} %copy.72), dimensions={0,2} | broadcast | bytes 18350080 | tf_op jit(solution)/shard_map/broadcast_in_dim | solution.py:95
  203.3 18.4 %convert_element_type.75 = f32[768,5120]{1,0:T(8,128)} reshape(f32[128,6,5120]{2,1,0:T(8,128)} %broadcast_in_dim.20) | data formatting | bytes 31457280 | tf_op jit(solution)/shard_map/convert_element_type | solution.py:95
  231.9 22.8 %gather_fusion = bf16[1024,5120]{1,0:T(8,128)(2,1)} fusion(bf16[769,5120]{1,0:T(8,128)(2,1)} %concatenate.15, s32[1024]{0:T(1024)S(1)} %get-tuple-element.6), kind=kCustom, calls=%fused_computation | custom fusion | bytes 20975616 | tf_op jit(solution)/shard_map/gather | solution.py:100
  254.7 74.7 %all-to-all-done.2 = bf16[16,2,32,5120]{3,2,1,0:T(8,128)(2,1)} async-done(((bf16[16,2,32,5120]{3,2,1,0:T(8,128)(2,1)}), bf16[16,2,32,5120]{3,2,1,0:T(8,128)(2,1)}, u32[]{:S(2)}, u32[]{:S(2)}) %all-to-all-start.2) | async-done | bytes 10485792 | tf_op jit(solution)/shard_map/all_to_all | solution.py:104
  334.3 7.0 fusion.33
  341.3 7.8 fusion.28
  349.1 126.2 %all-to-all-done.1 = bf16[16,2,32,5120]{3,2,1,0:T(8,128)(2,1)} async-done(((bf16[16,2,32,5120]{3,2,1,0:T(8,128)(2,1)}), bf16[16,2,32,5120]{3,2,1,0:T(8,128)(2,1)}, u32[]{:S(2)}, u32[]{:S(2)}) %all-to-all-start.1) | async-done | bytes 10485792 | tf_op jit(solution)/shard_map/all_to_all | solution.py:105
  475.3 8.7 %multiply_convert_fusion.2 = (bf16[16,2,32,192]{3,2,0,1:T(8,128)(2,1)S(1)}, bf16[16,2,32,192]{3,2,0,1:T(8,128)(2,1)S(1)}) fusion(f32[16,2,32,192]{3,2,0,1:T(8,128)S(1)} %fusion.33, f32[16,2,32,192]{3,2,0,1:T(8,128)} %fusion.28, bf16[2,192,5120]{2,1,0:T(8,128)(2,1)} %param.22, bf16[16,2,32,5120]{3,2,1,0:T(8,128)(2,1)} %all-to-all-done.1), kind=kOutput, calls=%fused_computation.43 | convolution fusion | flops 2015821824 | bytes 16777216 | tf_op jit(solution)/shard_map/secd,efd->secf/dot_general | solution.py:112
  484.0 8.5 %fusion.15 = f32[2,16,32,5120]{3,2,1,0:T(8,128)} fusion(bf16[16,2,32,192]{3,2,0,1:T(8,128)(2,1)S(1)} %get-tuple-element.5, bf16[2,192,5120]{2,1,0:T(8,128)(2,1)S(1)} %copy-done), kind=kOutput, calls=%fused_computation.22 | convolution fusion | flops 2013265920 | bytes 25296896 | tf_op jit(solution)/shard_map/secf,efd->secd/dot_general | solution.py:126
  492.6 13.2 %fusion.5 = bf16[16,2,32,5120]{3,2,0,1:T(8,128)(2,1)} fusion(f32[2,16,32,5120]{3,2,1,0:T(8,128)} %fusion.15, bf16[16,2,32,192]{3,2,0,1:T(8,128)(2,1)S(1)} %get-tuple-element.4, bf16[2,192,5120]{2,1,0:T(8,128)(2,1)} %param.21), kind=kOutput, calls=%fused_computation.11 | convolution fusion | flops 2023751680 | bytes 35782656 | tf_op jit(solution)/shard_map/secf,efd->secd/dot_general | solution.py:129
  505.7 9.0 %copy.95 = bf16[16,2,32,5120]{3,2,1,0:T(8,128)(2,1)} copy(bf16[16,2,32,5120]{3,2,0,1:T(8,128)(2,1)} %fusion.5) | data formatting | bytes 20971520 | tf_op jit(solution)/shard_map/convert_element_type | solution.py:132
  519.7 8.2 %bitcast_convert_fusion.1 = bf16[2,192,5120]{2,1,0:T(8,128)(2,1)} fusion(bf16[16,2,32,192]{3,2,0,1:T(8,128)(2,1)S(1)} %get-tuple-element.4, bf16[16,2,32,5120]{3,2,1,0:T(8,128)(2,1)} %all-to-all-done.2), kind=kOutput, calls=%fused_computation.13 | convolution fusion | flops 2015232000 | bytes 14811136 | tf_op jit(solution)/shard_map/secf,secd->efd/dot_general | solution.py:123
  527.9 132.6 %all-to-all-done.3 = bf16[16,2,32,5120]{3,2,1,0:T(8,128)(2,1)} async-done(((bf16[16,2,32,5120]{3,2,1,0:T(8,128)(2,1)}), bf16[16,2,32,5120]{3,2,1,0:T(8,128)(2,1)}, u32[]{:S(2)}, u32[]{:S(2)}) %all-to-all-start.3) | async-done | bytes 10485792 | tf_op jit(solution)/shard_map/all_to_all | solution.py:133
  660.5 20.3 %gather_fusion.2 = bf16[768,5120]{1,0:T(8,128)(2,1)} fusion(bf16[1024,5120]{1,0:T(8,128)(2,1)} %bitcast.22, s32[1024]{0:T(1024)S(1)} %pad_clamp_fusion), kind=kCustom, calls=%fused_computation.2 | custom fusion | bytes 15731712 | tf_op jit(solution)/shard_map/gather | solution.py:134
  680.8 13.1 %gather.14 = bf16[128,6,5120]{2,1,0:T(8,128)(2,1)} reshape(bf16[768,5120]{1,0:T(8,128)(2,1)} %gather_fusion.2) | data formatting | bytes 15728640 | tf_op jit(solution)/shard_map/gather | solution.py:134
  693.9 10.4 %reduce_sum.42 = bf16[128,5120]{1,0:T(8,128)(2,1)S(1)} reduce(bf16[128,6,5120]{2,1,0:T(8,128)(2,1)} %gather.14, bf16[]{:T(256)} %constant.25.clone.1), dimensions={1}, to_apply=%region_7.8 | reduce | flops 3276800 | bytes 9175042 | tf_op jit(solution)/shard_map/reduce_sum | solution.py:136
  706.0 8.2 %bitcast_convert_fusion.2 = bf16[2,192,5120]{2,1,0:T(8,128)(2,1)} fusion(bf16[16,2,32,192]{3,2,0,1:T(8,128)(2,1)S(1)} %get-tuple-element.5, bf16[16,2,32,5120]{3,2,1,0:T(8,128)(2,1)} %all-to-all-done.2), kind=kOutput, calls=%fused_computation.14 | convolution fusion | flops 2015232000 | bytes 14811136 | tf_op jit(solution)/shard_map/secf,secd->efd/dot_general | solution.py:120
  714.3 8.3 %bitcast_convert_fusion = bf16[2,192,5120]{2,1,0:T(8,128)(2,1)} fusion(bf16[16,2,32,5120]{3,2,1,0:T(8,128)(2,1)} %all-to-all-done.1, f32[16,2,32,192]{3,2,0,1:T(8,128)S(1)} %copy-done.11, f32[16,2,32,192]{3,2,0,1:T(8,128)S(1)} %fusion.33), kind=kOutput, calls=%fused_computation.12 | convolution fusion | flops 2016411648 | bytes 15990784 | tf_op jit(solution)/shard_map/secf,secd->efd/dot_general | solution.py:117
  722.6 55.7 %reduce-scatter.4.cloned.1.call-done = bf16[640,128]{1,0:T(8,128)(2,1)} async-done(((bf16[5120,128]{1,0:T(8,128)(2,1)}), bf16[640,128]{1,0:T(8,128)(2,1)}) %reduce-scatter.4.cloned.1.call-update) | async-done | bytes 163856
  (123 shorter events, 122.4 us)
Async XLA Ops:
  7.2 60.0 %copy-start.3 = (bf16[128,640]{1,0:T(8,128)(2,1)S(1)}, bf16[128,640]{1,0:T(8,128)(2,1)}, u32[]{:S(2)}) copy-start(bf16[128,640]{1,0:T(8,128)(2,1)} %param.15) | copy-start | bytes 491524
  7.2 150.2 %all-gather.2.cloned.1.call-start = ((), (), s32[]{:S(2)}) async-start(), calls=%async_computation.5 | async-start | bytes 1474560 | tf_op jit(solution)/shard_map/all_gather | solution.py:84
  8.3 81.8 %collective-permute-start.15 = (bf16[128,640]{0,1:T(8,128)(2,1)S(1)}, bf16[128,640]{0,1:T(8,128)(2,1)S(1)}, u32[]{:S(2)}, u32[]{:S(2)}) collective-permute-start(bf16[128,640]{0,1:T(8,128)(2,1)S(1)} %copy.79), channel_id=1, source_target_pairs={{0,8},{8,16},{16,24},{24,32},{32,40},{40,48},{48,56},{56,64},{64,7... | collective-permute-start | bytes 491528 | tf_op jit(solution)/shard_map/ppermute | solution.py:15
  9.6 79.8 %collective-permute-start.14 = (bf16[128,640]{0,1:T(8,128)(2,1)S(1)}, bf16[128,640]{0,1:T(8,128)(2,1)S(1)}, u32[]{:S(2)}, u32[]{:S(2)}) collective-permute-start(bf16[128,640]{0,1:T(8,128)(2,1)S(1)} %copy.79), channel_id=1, source_target_pairs={{0,16},{8,24},{16,32},{24,40},{32,48},{40,56},{48,64},{56,72},{64,... | collective-permute-start | bytes 491528 | tf_op jit(solution)/shard_map/ppermute | solution.py:15
  13.7 74.1 %collective-permute-start.13 = (bf16[128,640]{0,1:T(8,128)(2,1)S(1)}, bf16[128,640]{0,1:T(8,128)(2,1)S(1)}, u32[]{:S(2)}, u32[]{:S(2)}) collective-permute-start(bf16[128,640]{0,1:T(8,128)(2,1)S(1)} %copy.79), channel_id=1, source_target_pairs={{0,24},{8,32},{16,40},{24,48},{32,56},{40,64},{48,72},{56,80},{64,... | collective-permute-start | bytes 491528 | tf_op jit(solution)/shard_map/ppermute | solution.py:15
  17.8 13.0 %collective-permute-start.1 = (bf16[128,640]{1,0:T(8,128)(2,1)}, bf16[128,640]{1,0:T(8,128)(2,1)S(1)}, u32[]{:S(2)}, u32[]{:S(2)}) collective-permute-start(bf16[128,640]{1,0:T(8,128)(2,1)} %param.15), channel_id=1, source_target_pairs={{0,56},{8,64},{16,72},{24,80},{32,88},{40,96},{48,104},{56,112},{6... | collective-permute-start | bytes 491528 | tf_op jit(solution)/shard_map/ppermute | solution.py:15
  22.5 7.0 collective-permute-start
  29.5 7.9 %collective-permute-start.2 = (bf16[128,640]{1,0:T(8,128)(2,1)}, bf16[128,640]{1,0:T(8,128)(2,1)S(1)}, u32[]{:S(2)}, u32[]{:S(2)}) collective-permute-start(bf16[128,640]{1,0:T(8,128)(2,1)} %param.15), channel_id=1, source_target_pairs={{0,48},{8,56},{16,64},{24,72},{32,80},{40,88},{48,96},{56,104},{64... | collective-permute-start | bytes 491528 | tf_op jit(solution)/shard_map/ppermute | solution.py:15
  30.8 11.1 %collective-permute-start.3 = (bf16[128,640]{1,0:T(8,128)(2,1)}, bf16[128,640]{1,0:T(8,128)(2,1)S(1)}, u32[]{:S(2)}, u32[]{:S(2)}) collective-permute-start(bf16[128,640]{1,0:T(8,128)(2,1)} %param.15), channel_id=1, source_target_pairs={{0,40},{8,48},{16,56},{24,64},{32,72},{40,80},{48,88},{56,96},{64,... | collective-permute-start | bytes 491528 | tf_op jit(solution)/shard_map/ppermute | solution.py:15
  37.4 8.5 %collective-permute-start.4 = (bf16[128,640]{1,0:T(8,128)(2,1)}, bf16[128,640]{1,0:T(8,128)(2,1)S(1)}, u32[]{:S(2)}, u32[]{:S(2)}) collective-permute-start(bf16[128,640]{1,0:T(8,128)(2,1)} %param.15), channel_id=1, source_target_pairs={{0,32},{8,40},{16,48},{24,56},{32,64},{40,72},{48,80},{56,88},{64,... | collective-permute-start | bytes 491528 | tf_op jit(solution)/shard_map/ppermute | solution.py:15
  41.9 8.4 %collective-permute-start.5 = (bf16[128,640]{1,0:T(8,128)(2,1)}, bf16[128,640]{1,0:T(8,128)(2,1)S(1)}, u32[]{:S(2)}, u32[]{:S(2)}) collective-permute-start(bf16[128,640]{1,0:T(8,128)(2,1)} %param.15), channel_id=1, source_target_pairs={{0,24},{8,32},{16,40},{24,48},{32,56},{40,64},{48,72},{56,80},{64,... | collective-permute-start | bytes 491528 | tf_op jit(solution)/shard_map/ppermute | solution.py:15
  46.0 8.6 %collective-permute-start.6 = (bf16[128,640]{1,0:T(8,128)(2,1)}, bf16[128,640]{1,0:T(8,128)(2,1)S(1)}, u32[]{:S(2)}, u32[]{:S(2)}) collective-permute-start(bf16[128,640]{1,0:T(8,128)(2,1)} %param.15), channel_id=1, source_target_pairs={{0,16},{8,24},{16,32},{24,40},{32,48},{40,56},{48,64},{56,72},{64,... | collective-permute-start | bytes 491528 | tf_op jit(solution)/shard_map/ppermute | solution.py:15
  50.3 12.3 %collective-permute-start.7 = (bf16[128,640]{1,0:T(8,128)(2,1)}, bf16[128,640]{1,0:T(8,128)(2,1)S(1)}, u32[]{:S(2)}, u32[]{:S(2)}) collective-permute-start(bf16[128,640]{1,0:T(8,128)(2,1)} %param.15), channel_id=1, source_target_pairs={{0,8},{8,16},{16,24},{24,32},{32,40},{40,48},{48,56},{56,64},{64,7... | collective-permute-start | bytes 491528 | tf_op jit(solution)/shard_map/ppermute | solution.py:15
  54.6 19.2 %collective-permute-start.9 = (bf16[128,640]{0,1:T(8,128)(2,1)S(1)}, bf16[128,640]{0,1:T(8,128)(2,1)S(1)}, u32[]{:S(2)}, u32[]{:S(2)}) collective-permute-start(bf16[128,640]{0,1:T(8,128)(2,1)S(1)} %copy.79), channel_id=1, source_target_pairs={{0,56},{8,64},{16,72},{24,80},{32,88},{40,96},{48,104},{56,112},{6... | collective-permute-start | bytes 491528 | tf_op jit(solution)/shard_map/ppermute | solution.py:15
  62.6 9.2 %collective-permute-start.8 = (bf16[128,640]{0,1:T(8,128)(2,1)S(1)}, bf16[128,640]{0,1:T(8,128)(2,1)S(1)}, u32[]{:S(2)}, u32[]{:S(2)}) collective-permute-start(bf16[128,640]{0,1:T(8,128)(2,1)S(1)} %copy.79), channel_id=1, source_target_pairs={{0,64},{8,72},{16,80},{24,88},{32,96},{40,104},{48,112},{56,120},{... | collective-permute-start | bytes 491528 | tf_op jit(solution)/shard_map/ppermute | solution.py:15
  71.8 7.7 collective-permute-start.10
  73.8 11.2 %collective-permute-start.11 = (bf16[128,640]{0,1:T(8,128)(2,1)S(1)}, bf16[128,640]{0,1:T(8,128)(2,1)S(1)}, u32[]{:S(2)}, u32[]{:S(2)}) collective-permute-start(bf16[128,640]{0,1:T(8,128)(2,1)S(1)} %copy.79), channel_id=1, source_target_pairs={{0,40},{8,48},{16,56},{24,64},{32,72},{40,80},{48,88},{56,96},{64,... | collective-permute-start | bytes 491528 | tf_op jit(solution)/shard_map/ppermute | solution.py:15
  79.5 7.7 collective-permute-start.12
  98.3 60.8 %copy-start.6 = (f32[5120]{0:T(1024)S(1)}, f32[5120]{0:T(1024)}, u32[]{:S(2)}) copy-start(f32[5120]{0:T(1024)} %param.17) | copy-start | bytes 61444
  99.4 70.2 %all-to-all-start = ((bf16[8,128,640]{2,1,0:T(8,128)(2,1)}), bf16[8,128,640]{2,1,0:T(8,128)(2,1)S(1)}, u32[]{:S(2)}, u32[]{:S(2)}) async-start(bf16[8,128,640]{2,1,0:T(8,128)(2,1)} %stack.2), calls=%async_computation | async-start | bytes 2621440 | tf_op jit(solution)/shard_map/all_to_all | solution.py:86
  169.7 159.7 %all-to-all-start.2 = ((bf16[16,2,32,5120]{3,2,1,0:T(8,128)(2,1)}), bf16[16,2,32,5120]{3,2,1,0:T(8,128)(2,1)}, u32[]{:S(2)}, u32[]{:S(2)}) async-start(bf16[16,2,32,5120]{3,2,1,0:T(8,128)(2,1)} %bitcast.98), calls=%async_computation.2 | async-start | bytes 20971520 | tf_op jit(solution)/shard_map/all_to_all | solution.py:104
  329.4 145.9 %all-to-all-start.1 = ((bf16[16,2,32,5120]{3,2,1,0:T(8,128)(2,1)}), bf16[16,2,32,5120]{3,2,1,0:T(8,128)(2,1)}, u32[]{:S(2)}, u32[]{:S(2)}) async-start(bf16[16,2,32,5120]{3,2,1,0:T(8,128)(2,1)} %bitcast.99), calls=%async_computation.1 | async-start | bytes 20971520 | tf_op jit(solution)/shard_map/all_to_all | solution.py:105
  514.7 145.8 %all-to-all-start.3 = ((bf16[16,2,32,5120]{3,2,1,0:T(8,128)(2,1)}), bf16[16,2,32,5120]{3,2,1,0:T(8,128)(2,1)}, u32[]{:S(2)}, u32[]{:S(2)}) async-start(bf16[16,2,32,5120]{3,2,1,0:T(8,128)(2,1)} %copy.95), calls=%async_computation.3 | async-start | bytes 20971520 | tf_op jit(solution)/shard_map/all_to_all | solution.py:133
  519.7 258.7 %reduce-scatter.4.cloned.1.call-start = ((), (), s32[]{:S(2)}) async-start(), calls=%async_computation.6 | async-start | bytes 1474560
  (10 other events, 117.1 us)
Sparse Core Ops, SparseCore 0:
  98.4 58.9 all-gather.1
  706.1 72.1 reduce-scatter.3
